TPU v7x, 128 devices: a whole 4x4x4 slice. The times are simulated.
128 devices in a mesh: sink: 8 (over x, z_hi), src: 16 (over z_lo, y, core).
Axes of the slice: x: 4, y: 4, z: 4 (z_hi: 2, z_lo: 2; z = z_hi * 2 + z_lo), core: 2. Of those that a mesh axis runs over, the one named last changes fastest.
Arguments:
- perambulator: bfloat16 [2, 16, 32, 512, 512], P(None, None, 'src', None, 'sink'), may hold values from -6 to 6
- elementals: bfloat16 [2, 16, 8, 512, 512], P(None, 'sink', None, 'src'), may hold values from -0.1875 to 0.1875
- op_ids: int32 [16, 8], P('sink'), may hold values from 0 to 7, each once within a row
Outputs:
- products: bfloat16 [2, 4, 16, 32, 512, 512], P(None, None, 'sink', 'src')
Inputs may be any that keep to these rules, and one draw needn't show every extreme that they name: `op_ids`: each row is a permutation of 0 to 7.
All inputs are finite; a program needn't handle non-finite values.
Results may differ from a plain program's by a relative error of at most 0.001.
Values may be sent and summed in bfloat16 or wider, within the bound.
A program may use at most 128 MiB of HBM per device.

v0:
```python
import jax
import jax.numpy as jnp
from jax import lax
from jax.sharding import PartitionSpec as P

NOP = 4


def select_ops(bank, op_ids):
    wanted = op_ids[:, :NOP]
    table = (
        wanted[:, :, None] == jnp.arange(bank.shape[2], dtype=jnp.int32)[None, None, :]
    ).astype(jnp.bfloat16)
    return jnp.einsum("tob,ctbrv->ctorv", table, bank, preferred_element_type=jnp.float32).astype(
        jnp.bfloat16
    )


def shards(perambulator, elementals, op_ids):
    local = lax.all_to_all(perambulator, "sink", split_axis=1, concat_axis=4, tiled=True)
    whole = lax.all_gather(elementals, "src", axis=3, tiled=True)
    piece = select_ops(whole, op_ids)
    real_part = jnp.einsum(
        "torv,tsvw->otsrw", piece[0], local[0], preferred_element_type=jnp.float32
    ) - jnp.einsum("torv,tsvw->otsrw", piece[1], local[1], preferred_element_type=jnp.float32)
    imag_part = jnp.einsum(
        "torv,tsvw->otsrw", piece[0], local[1], preferred_element_type=jnp.float32
    ) + jnp.einsum("torv,tsvw->otsrw", piece[1], local[0], preferred_element_type=jnp.float32)
    return jnp.stack([real_part, imag_part]).astype(jnp.bfloat16)


def solution(mesh):
    in_specs = (
        P(None, None, "src", None, "sink"),
        P(None, "sink", None, "src", None),
        P("sink", None),
    )
    out_specs = P(None, None, "sink", "src", None, None)
    return jax.shard_map(shards, mesh=mesh, in_specs=in_specs, out_specs=out_specs, check_vma=False)
```

profile of v0, /device:TPU:1, one launch (start us, length us, event | category | flops | bytes accessed | tf_op | source)
XLA Modules:
  0.0 227.8 jit_solution(4542009888599747)
XLA Ops:
  6.5 0.0 all-gather.2.cloned.1.call-start
  6.5 2.8 %copy.33 = bf16[2,2,8,32,512]{4,2,3,0,1:T(8,128)(2,1)} copy(bf16[2,2,8,32,512]{4,3,2,1,0:T(8,128)(2,1)} %param.4) | data formatting | bytes 2097152 | tf_op args[1]
  9.3 0.0 all-gather.2.cloned.1.call-update
  9.3 2.7 %copy.34 = bf16[2,16,2,512,64]{3,4,2,0,1:T(8,128)(2,1)S(1)} copy(bf16[2,16,2,512,64]{3,4,2,1,0:T(8,128)(2,1)} %param.3) | data formatting | bytes 8388608 | tf_op args[0]
  12.0 64.5 %all_to_all.15 = bf16[2,16,2,512,64]{3,4,2,0,1:T(8,128)(2,1)S(1)} all-to-all(bf16[2,16,2,512,64]{3,4,2,0,1:T(8,128)(2,1)S(1)} %copy.34), channel_id=1, replica_groups=mesh['sink'=8,'src'=16] {'sink'}, dimensions={1} | all-to-all | bytes 8388608 | tf_op jit(solution)/shard_map/all_to_all | solution.py:20
  76.5 0.5 copy.35
  77.0 0.4 fusion.11
  77.3 0.0 copy-start.1
  77.4 0.2 copy.36
  77.6 1.5 copy.39
  79.0 68.7 %all-gather.2.cloned.1.call-done = bf16[2,2,8,512,512]{4,2,3,0,1:T(8,128)(2,1)} async-done(((bf16[2,2,8,32,512]{4,2,3,0,1:T(8,128)(2,1)}), bf16[2,2,8,512,512]{4,2,3,0,1:T(8,128)(2,1)}) %all-gather.2.cloned.1.call-update) | async-done | bytes 16777232 | tf_op jit(solution)/shard_map/all_gather | solution.py:21
  147.8 0.0 copy-done.1
  147.8 8.5 %convert_bitcast_fusion = bf16[2,2,4,512,512]{4,2,3,0,1:T(4,128)(2,1)S(1)} fusion(bf16[2,2,8,512,512]{4,2,3,0,1:T(8,128)(2,1)} %all-gather.2.cloned.1.call-done, s32[2,4]{1,0:T(2,128)S(1)} %bitcast.51), kind=kOutput, calls=%fused_computation.5 | convolution fusion | flops 71303232 | bytes 25165856 | tf_op jit(solution)/shard_map/tob,ctbrv->ctorv/dot_general | solution.py:14
  156.3 0.0 copy-start
  156.4 4.3 %slice_bitcast_fusion = (bf16[2,4,512,512,1]{3,1,2,0,4:T(4,128)(2,1)}, bf16[2,4,512,512,1]{3,1,2,0,4:T(4,128)(2,1)S(1)}) fusion(bf16[2,2,4,512,512]{4,2,3,0,1:T(4,128)(2,1)S(1)} %convert_bitcast_fusion), kind=kLoop, calls=%fused_computation.6 | loop fusion | bytes 16777216 | tf_op jit(solution)/shard_map/squeeze | solution.py:25
  160.6 0.0 copy-done
  160.6 8.6 %fusion.4 = f32[2,4,512,2,512]{4,2,3,1,0:T(8,128)} fusion(bf16[2,2,512,512,1]{2,3,1,4,0:T(8,128)(2,1)S(1)} %bitcast.50, bf16[2,4,512,512,1]{3,1,2,0,4:T(4,128)(2,1)S(1)} %get-tuple-element.6), kind=kOutput, calls=%fused_computation.10 | convolution fusion | flops 4294967296 | bytes 23068672 | tf_op jit(solution)/shard_map/torv,tsvw->otsrw/dot_general | solution.py:26
  169.2 8.2 %fusion.6 = f32[2,4,512,2,512]{4,2,3,1,0:T(8,128)} fusion(bf16[2,2,512,512,1]{2,3,1,4,0:T(8,128)(2,1)S(1)} %bitcast.47, bf16[2,4,512,512,1]{3,1,2,0,4:T(4,128)(2,1)S(1)} %get-tuple-element.6), kind=kOutput, calls=%fused_computation.12 | convolution fusion | flops 4294967296 | bytes 23068672 | tf_op jit(solution)/shard_map/torv,tsvw->otsrw/dot_general | solution.py:23
  177.4 13.2 %fusion.1 = bf16[1,4,2,2,512,512]{5,4,3,1,2,0:T(8,128)(2,1)} fusion(f32[2,4,512,2,512]{4,2,3,1,0:T(8,128)} %fusion.4, bf16[2,2,512,512,1]{2,3,1,4,0:T(8,128)(2,1)S(1)} %bitcast.48, bf16[2,4,512,512,1]{3,1,2,0,4:T(4,128)(2,1)} %get-tuple-element.5), kind=kOutput, calls=%fused_computation.4 | convolution fusion | flops 4303355904 | bytes 31457280 | tf_op jit(solution)/shard_map/torv,tsvw->otsrw/dot_general | solution.py:28
  190.6 15.8 %fusion = bf16[1,4,2,2,512,512]{5,4,3,1,2,0:T(8,128)(2,1)} fusion(f32[2,4,512,2,512]{4,2,3,1,0:T(8,128)} %fusion.6, bf16[2,2,512,512,1]{2,3,1,4,0:T(8,128)(2,1)} %bitcast.49, bf16[2,4,512,512,1]{3,1,2,0,4:T(4,128)(2,1)} %get-tuple-element.5), kind=kOutput, calls=%fused_computation.3 | convolution fusion | flops 4303355904 | bytes 31457280 | tf_op jit(solution)/shard_map/torv,tsvw->otsrw/dot_general | solution.py:25
  206.3 8.0 %pad_maximum_fusion = bf16[2,4,2,2,512,512]{5,4,3,1,2,0:T(8,128)(2,1)S(1)} fusion(bf16[1,4,2,2,512,512]{5,4,3,1,2,0:T(8,128)(2,1)} %fusion.1, bf16[1,4,2,2,512,512]{5,4,3,1,2,0:T(8,128)(2,1)} %fusion), kind=kLoop, calls=%fused_computation | loop fusion | flops 8388608 | bytes 33554432 | tf_op jit(solution)/shard_map/stack | solution.py:29
  214.4 6.5 %copy.46 = bf16[2,4,2,2,512,512]{5,4,3,2,1,0:T(8,128)(2,1)} copy(bf16[2,4,2,2,512,512]{5,4,3,1,2,0:T(8,128)(2,1)S(1)} %pad_maximum_fusion) | data formatting | bytes 33554432 | tf_op jit(solution)/shard_map/stack | solution.py:29
Async XLA Ops:
  6.5 141.3 %all-gather.2.cloned.1.call-start = ((), (), s32[]{:S(2)}) async-start(), calls=%async_computation.1 | async-start | bytes 17825792 | tf_op jit(solution)/shard_map/all_gather | solution.py:21
  77.3 70.5 %copy-start.1 = (s32[2,8]{1,0:T(2,128)S(1)}, s32[2,8]{1,0:T(2,128)}, u32[]{:S(2)}) copy-start(s32[2,8]{1,0:T(2,128)} %param.5) | copy-start | bytes 196
  156.3 4.3 %copy-start = (bf16[1,2,2,512,8,64]{3,5,4,2,1,0:T(8,128)(2,1)S(1)}, bf16[1,2,2,512,8,64]{3,5,4,2,1,0:T(8,128)(2,1)}, u32[]{:S(2)}) copy-start(bf16[1,2,2,512,8,64]{3,5,4,2,1,0:T(8,128)(2,1)} %copy.39) | copy-start | bytes 6291460
Sparse Core Ops, SparseCore 0:
  9.5 138.2 all-gather.1
where the time goes:
time: 228 us
  waiting for transfers between devices  68.8 us (30%)
  blocking collectives  64.5 us (28%)
  matrix products  54.3 us (24%)
  local copies, waits for them, and re-layouts  18.8 us (8%)
  between operations  13.5 us (6%)
  other arithmetic  8 us (4%)
    all_gather x1, waiting for transfers between devices, shards(): whole = lax.all_gather(elementals, 'src', axis=3, tiled=True)  68.7 us
    all_to_all x1, blocking collectives, shards(): lax.all_to_all(perambulator, 'sink', split_axis=1, concat_axis=4, tiled=T...  64.5 us
    dot_general x1, matrix products, shards(): jnp.einsum('torv,tsvw->otsrw', piece[1], local[1], preferred_element_type...  15.8 us
    dot_general x1, matrix products, shards(): jnp.einsum('torv,tsvw->otsrw', piece[1], local[0], preferred_element_type...  13.2 us
    dot_general x1, matrix products, shards(): jnp.einsum('torv,tsvw->otsrw', piece[0], local[1], preferred_element_type...  8.59 us
    dot_general x1, matrix products, select_ops(): jnp.einsum('tob,ctbrv->ctorv', table, bank, preferred_element_type=jnp.fl...  8.54 us
    dot_general x1, matrix products, shards(): jnp.einsum('torv,tsvw->otsrw', piece[0], local[0], preferred_element_type...  8.16 us
    another operation x1, other arithmetic, shards(): return jnp.stack([real_part, imag_part]).astype(jnp.bfloat16)  8 us
  transfers between devices with their start and end apart: 1, of which 1 were waited for; matrix products, arithmetic and copies ran while one was open for 2% of the time, Pallas kernels for 0%

commit v1 on v0

v1 whole, which is shorter than its diff:
```python
import functools

import jax
import jax.numpy as jnp
from jax import lax
from jax.experimental import pallas as pl
from jax.experimental.pallas import tpu as pltpu
from jax.sharding import PartitionSpec as P

NOP = 4
MESH = pl.DeviceIdType.MESH
HOPS = ((1, 0), (3, 0), (0, 1), (2, 0), (1, 1), (3, 1), (2, 1))
BF16 = jnp.bfloat16


def kernel(ids, stored, peram, out, bank, ops, cols, weights, load_sem, own_sem, p_send, p_recv, z_send, z_recv, y_send, y_recv, c_send, c_recv):
    sink, src = lax.axis_index("sink"), lax.axis_index("src")
    x, zh = sink // 2, sink % 2
    zl, y, core = src // 8, (src // 2) % 4, src % 2

    def sink_of(dx, dz):
        return lax.rem(x + dx, 4) * 2 + lax.rem(zh + dz, 2)

    def src_of(dl, dy, dc):
        return lax.rem(zl + dl, 2) * 8 + lax.rem(y + dy, 4) * 2 + lax.rem(core + dc, 2)

    load = pltpu.make_async_copy(stored, bank, load_sem)
    load.start()

    barrier = pltpu.get_barrier_semaphore()
    partners = [(sink_of(dx, dz), src) for dx, dz in HOPS]
    partners += [(sink, src_of(0, dy, 0)) for dy in (1, 2, 3)]
    partners += [(sink, src_of(1, 0, 0)), (sink, src_of(0, 0, 1))]
    for partner in partners:
        pl.semaphore_signal(barrier, inc=1, device_id=partner, device_id_type=MESH)

    load.wait()
    rows = pl.ds(pl.multiple_of(src * 32, 32), 32)
    for t in range(2):
        for o in range(NOP):
            which = ids[t, o]
            for c in range(2):
                ops[t, o, rows, c * 512 : (c + 1) * 512] = bank[c, t, which]

    pl.semaphore_wait(barrier, len(partners))

    def rows_of(block):
        return pl.ds(pl.multiple_of(block * 32, 32), 32)

    def op_copy(block, t, send, recv, target):
        piece = ops.at[t, :, rows_of(block), :]
        return pltpu.make_async_remote_copy(
            src_ref=piece, dst_ref=piece, send_sem=send, recv_sem=recv, device_id=(sink, target), device_id_type=MESH
        )

    def z_copy(t, arriving=False):
        return op_copy(src_of(1, 0, 0) if arriving else src, t, z_send.at[t], z_recv.at[t], src_of(1, 0, 0))

    def y_copy(h, dy, t, arriving=False):
        block = src_of(h, 4 - dy, 0) if arriving else src_of(h, 0, 0)
        return op_copy(block, t, y_send.at[h, dy - 1, t], y_recv.at[h, dy - 1, t], src_of(0, dy, 0))

    def c_copy(h, dy, t, arriving=False):
        block = src_of(h, 4 - dy, 1 if arriving else 0)
        return op_copy(block, t, c_send.at[h, dy, t], c_recv.at[h, dy, t], src_of(0, 0, 1))

    def p_copy(k, t, s, arriving=False):
        dx, dz = HOPS[k]
        target = sink_of(dx, dz)
        owner = sink_of(4 - dx, dz) if arriving else sink
        return pltpu.make_async_remote_copy(
            src_ref=peram.at[:, 2 * target + t, s],
            dst_ref=cols.at[t, s, :, pl.ds(pl.multiple_of(owner * 64, 64), 64), :],
            send_sem=p_send.at[k, t, s],
            recv_sem=p_recv.at[k, t, s],
            device_id=(target, src),
            device_id_type=MESH,
        )

    def own_copy(t, s):
        return pltpu.make_async_copy(
            peram.at[:, 2 * sink + t, s],
            cols.at[t, s, :, pl.ds(pl.multiple_of(sink * 64, 64), 64), :],
            own_sem.at[t, s],
        )

    for t in range(2):
        z_copy(t).start()
    for t in range(2):
        for dy in (1, 3, 2):
            y_copy(0, dy, t).start()
        c_copy(0, 0, t).start()
    for t in range(2):
        for s in range(2):
            for k in range(7):
                p_copy(k, t, s).start()
            own_copy(t, s).start()

    for t in range(2):
        z_copy(t, True).wait_recv()
        for dy in (1, 3, 2):
            y_copy(1, dy, t).start()
        c_copy(1, 0, t).start()
    for h in range(2):
        for t in range(2):
            for dy in (1, 3, 2):
                y_copy(h, dy, t, True).wait_recv()
                c_copy(h, dy, t).start()
    for h in range(2):
        for t in range(2):
            for dy in range(4):
                c_copy(h, dy, t, True).wait_recv()

    def products(t, s, dx):
        first = pl.multiple_of(lax.rem(x + dx, 4) * 128, 128)
        real, imag = cols[t, s, 0, pl.ds(first, 128), :], cols[t, s, 1, pl.ds(first, 128), :]
        weights[0:128, 0:512] = real
        weights[0:128, 512:1024] = -imag
        weights[128:256, 0:512] = imag
        weights[128:256, 512:1024] = real

        def one(o, carry):
            both = lax.dot_general(
                ops[t, o], weights[...], (((1,), (1,)), ((), ())), preferred_element_type=jnp.float32
            ).astype(BF16)
            out[0, o, t, s, :, pl.ds(first, 128)] = both[:, 0:128]
            out[1, o, t, s, :, pl.ds(first, 128)] = both[:, 128:256]
            return carry

        lax.fori_loop(0, NOP, one, 0)

    for t in range(2):
        for s in range(2):
            for dx in (0, 3, 1, 2):
                for k, hop in enumerate(HOPS):
                    if hop[0] == (4 - dx) % 4:
                        p_copy(k, t, s, True).wait_recv()
                if dx == 0:
                    own_copy(t, s).wait()
                products(t, s, dx)

    for t in range(2):
        z_copy(t).wait_send()
        for h in range(2):
            for dy in range(1, 4):
                y_copy(h, dy, t).wait_send()
            for dy in range(4):
                c_copy(h, dy, t).wait_send()
        for s in range(2):
            for k in range(7):
                p_copy(k, t, s).wait_send()


def shards(perambulator, elementals, op_ids):
    peram = jnp.swapaxes(perambulator, 3, 4)
    dma = pltpu.SemaphoreType.DMA
    return pl.pallas_call(
        kernel,
        out_shape=pltpu.VMEM((2, NOP, 2, 2, 512, 512), BF16),
        in_specs=[
            pl.BlockSpec(memory_space=pltpu.SMEM),
            pl.BlockSpec(memory_space=pl.ANY),
            pl.BlockSpec(memory_space=pl.ANY),
        ],
        out_specs=pl.BlockSpec(memory_space=pltpu.VMEM),
        scratch_shapes=[
            pltpu.VMEM((2, 2, 8, 32, 512), BF16),
            pltpu.VMEM((2, NOP, 512, 1024), BF16),
            pltpu.VMEM((2, 2, 2, 512, 512), BF16),
            pltpu.VMEM((256, 1024), BF16),
            dma(()),
            dma((2, 2)),
            dma((7, 2, 2)),
            dma((7, 2, 2)),
            dma((2,)),
            dma((2,)),
            dma((2, 3, 2)),
            dma((2, 3, 2)),
            dma((2, 4, 2)),
            dma((2, 4, 2)),
        ],
        compiler_params=pltpu.CompilerParams(
            collective_id=0, has_side_effects=True, vmem_limit_bytes=40 * 2**20
        ),
    )(op_ids, elementals, peram)


def solution(mesh):
    in_specs = (
        P(None, None, "src", None, "sink"),
        P(None, "sink", None, "src", None),
        P("sink", None),
    )
    out_specs = P(None, None, "sink", "src", None, None)
    return jax.shard_map(shards, mesh=mesh, in_specs=in_specs, out_specs=out_specs, check_vma=False)
```

time: 228 us -> 97.6 us (0.43)
  Pallas kernels: 0 us -> 91.3 us
  waiting for transfers between devices: 68.8 us -> 0 us
  blocking collectives: 64.5 us -> 0 us
  matrix products: 54.3 us -> 0 us
  between operations: 13.5 us -> 0.01 us
  local copies, waits for them, and re-layouts: 18.8 us -> 6.16 us
  other arithmetic: 8 us -> 0 us
    pallas_call x0 -> x1, Pallas kernels: none -> 91.3 us  [shards(): pl.pallas_call(kernel, out_shape=pltpu.VMEM((2, NOP, 2, 2, 512, 512), BF1...]
    all_gather x1 -> x0, waiting for transfers between devices: 68.7 us -> none  [shards(): whole = lax.all_gather(elementals, 'src', axis=3, tiled=True)]
    all_to_all x1 -> x0, blocking collectives: 64.5 us -> none  [shards(): lax.all_to_all(perambulator, 'sink', split_axis=1, concat_axis=4, tiled=T...]
    dot_general x5 -> x0, matrix products: 54.3 us -> none  [the longest x1 15.8 us: shards(): jnp.einsum('torv,tsvw->otsrw', piece[1], local[1], preferred_element_type...]
    another operation x1 -> x0, other arithmetic: 8 us -> none  [shards(): return jnp.stack([real_part, imag_part]).astype(jnp.bfloat16)]
    another operation x1 -> x0, local copies, waits for them, and re-layouts: 6.55 us -> none  [shards(): return jnp.stack([real_part, imag_part]).astype(jnp.bfloat16)]
    squeeze x1 -> x0, local copies, waits for them, and re-layouts: 4.26 us -> none  [shards(): piece[1]]
    unnamed x6 -> x1, local copies, waits for them, and re-layouts: 5.46 us -> 6.16 us
  transfers between devices with their start and end apart: 1 -> 0, of which waited for: 1 -> 0; matrix products, arithmetic and copies ran while one was open for 2% -> 0% of each run, Pallas kernels for 0% -> 0%
where the time goes in v1:
time: 97.6 us; the launch traced here: 97.4 us
  Pallas kernels  91.3 us (94%)
  local copies, waits for them, and re-layouts  6.16 us (6%)
    pallas_call x1, Pallas kernels, shards(): pl.pallas_call(kernel, out_shape=pltpu.VMEM((2, NOP, 2, 2, 512, 512), BF1...  91.3 us
    unnamed x1, local copies, waits for them, and re-layouts  6.16 us

profile of v1, /device:TPU:1, one launch (start us, length us, event | category | flops | bytes accessed | tf_op | source)
XLA Modules:
  0.0 97.4 jit_solution(9774665688442793260)
XLA Ops:
  0.0 91.3 %shard_map.37 = bf16[2,4,2,2,512,512]{5,4,3,2,1,0:T(8,128)(2,1)S(1)} custom-call(s32[2,8]{1,0:T(2,128)} %ids.1, bf16[2,2,8,32,512]{4,3,2,1,0:T(8,128)(2,1)} %stored.1, bf16[2,16,2,64,512]{4,3,2,1,0:T(8,128)(2,1)} %bitcast.1), custom_call_target="tpu_custom_call" | custom-call | tf_op jit(solution)/shard_map/pallas_call | solution.py:157
  91.3 6.2 %copy.5 = bf16[2,4,2,2,512,512]{5,4,3,2,1,0:T(8,128)(2,1)} copy(bf16[2,4,2,2,512,512]{5,4,3,2,1,0:T(8,128)(2,1)S(1)} %shard_map.37) | data formatting | bytes 33554432

commit v2 on v1

v2 whole, which is shorter than its diff:
```python
import functools

import jax
import jax.numpy as jnp
from jax import lax
from jax.experimental import pallas as pl
from jax.experimental.pallas import tpu as pltpu
from jax.sharding import PartitionSpec as P

NOP = 4
MESH = pl.DeviceIdType.MESH
BF16 = jnp.bfloat16


def kernel(ids, stored, peram, out, ops, cols, bank, weights, load_sem, p_send, p_recv, z_send, z_recv, y_send, y_recv, f_send, f_recv, c_send, c_recv):
    sink, src = lax.axis_index("sink"), lax.axis_index("src")
    x, zh = sink // 2, sink % 2
    zl, y, core = src // 8, (src // 2) % 4, src % 2

    def sink_of(dx, dz):
        return lax.rem(x + dx, 4) * 2 + lax.rem(zh + dz, 2)

    def src_of(dl, dy, dc):
        return lax.rem(zl + dl, 2) * 8 + lax.rem(y + dy, 4) * 2 + lax.rem(core + dc, 2)

    load = pltpu.make_async_copy(stored, bank, load_sem)
    load.start()

    barrier = pltpu.get_barrier_semaphore()
    partners = [(sink_of(dx, dz), src) for dx in range(4) for dz in range(2) if dx or dz]
    partners += [(sink, src_of(0, dy, 0)) for dy in (1, 3)]
    partners += [(sink, src_of(1, 0, 0)), (sink, src_of(0, 0, 1))]
    for partner in partners:
        pl.semaphore_signal(barrier, inc=1, device_id=partner, device_id_type=MESH)

    load.wait()
    rows = pl.ds(pl.multiple_of(src * 32, 32), 32)
    for t in range(2):
        for o in range(NOP):
            which = ids[t, o]
            for c in range(2):
                ops[t, o, rows, c * 512 : (c + 1) * 512] = bank[c, t, which]

    pl.semaphore_wait(barrier, len(partners))

    def op_copy(block, t, send, recv, target, o=slice(0, NOP)):
        piece = ops.at[t, o, pl.ds(pl.multiple_of(block * 32, 32), 32), :]
        return pltpu.make_async_remote_copy(
            src_ref=piece, dst_ref=piece, send_sem=send, recv_sem=recv, device_id=(sink, target), device_id_type=MESH
        )

    def z_copy(t, arriving=False):
        return op_copy(src_of(1, 0, 0) if arriving else src, t, z_send.at[t], z_recv.at[t], src_of(1, 0, 0))

    def y_copy(h, way, t, arriving=False):
        back, to = (3, 1) if way == 0 else (1, 3)
        block = src_of(h, back if arriving else 0, 0)
        return op_copy(block, t, y_send.at[h, way, t], y_recv.at[h, way, t], src_of(0, to, 0))

    def f_copy(h, way, t, arriving=False):
        back, to = (3, 1) if way == 0 else (1, 3)
        block = src_of(h, 2 if arriving else back, 0)
        half = slice(2 * way, 2 * way + 2)
        return op_copy(block, t, f_send.at[h, way, t], f_recv.at[h, way, t], src_of(0, to, 0), half)

    def c_copy(h, dy, t, arriving=False):
        block = src_of(h, dy, 1 if arriving else 0)
        return op_copy(block, t, c_send.at[h, dy, t], c_recv.at[h, dy, t], src_of(0, 0, 1))

    def p_copy(dx, dz, t, s, arriving=False):
        target = sink_of(dx, dz)
        owner = sink_of(4 - dx, dz) if arriving else sink
        here = peram.at[:, 2 * target + t, s]
        there = cols.at[t, s, :, pl.ds(pl.multiple_of(owner * 64, 64), 64), :]
        if not arriving and dx == 0 and dz == 0:
            return pltpu.make_async_copy(here, there, p_recv.at[0, 0, t, s])
        return pltpu.make_async_remote_copy(
            src_ref=here,
            dst_ref=there,
            send_sem=p_send.at[dx, dz, t, s],
            recv_sem=p_recv.at[dx, dz, t, s],
            device_id=(target, src),
            device_id_type=MESH,
        )

    def send_own(t):
        for way in range(2):
            y_copy(0, way, t).start()
        c_copy(0, 0, t).start()

    def send_columns(dz, t, s):
        for dx in (0, 1, 3, 2):
            p_copy(dx, dz, t, s).start()

    def pass_on(h, t):
        for way in range(2):
            y_copy(h, way, t, True).wait_recv()
            f_copy(h, way, t).start()
            c_copy(h, 3 - 2 * way, t).start()

    z_copy(0).start()
    send_own(0)
    z_copy(1).start()
    send_own(1)
    send_columns(1, 0, 0)
    send_columns(0, 0, 0)
    for t in range(2):
        z_copy(t, True).wait_recv()
        for way in range(2):
            y_copy(1, way, t).start()
        c_copy(1, 0, t).start()
        pass_on(0, t)
    send_columns(1, 0, 1)
    send_columns(0, 0, 1)
    for t in range(2):
        pass_on(1, t)
    send_columns(1, 1, 0)
    send_columns(0, 1, 0)
    for h in range(2):
        for t in range(2):
            for way in range(2):
                f_copy(h, way, t, True).wait_recv()
            c_copy(h, 2, t).start()
    send_columns(1, 1, 1)
    send_columns(0, 1, 1)
    for h in range(2):
        for t in range(2):
            for dy in range(4):
                c_copy(h, dy, t, True).wait_recv()

    def products(i, carry):
        t, s, pair = i // 4, (i // 2) % 2, i % 2
        steps = (3 * pair, 1 + pair)
        firsts = [pl.multiple_of(lax.rem(x + 4 - dx, 4) * 128, 128) for dx in steps]
        for n, dx in enumerate(steps):
            for dz in range(2):
                p_copy(dx, dz, t, s, True).wait_recv()
        for n, first in enumerate(firsts):
            real, imag = cols[t, s, 0, pl.ds(first, 128), :], cols[t, s, 1, pl.ds(first, 128), :]
            weights[256 * n : 256 * n + 128, 0:512] = real
            weights[256 * n : 256 * n + 128, 512:1024] = -imag
            weights[256 * n + 128 : 256 * n + 256, 0:512] = imag
            weights[256 * n + 128 : 256 * n + 256, 512:1024] = real
        for o in range(NOP):
            result = lax.dot_general(
                ops[t, o], weights[...], (((1,), (1,)), ((), ())), preferred_element_type=jnp.float32
            ).astype(BF16)
            for n, first in enumerate(firsts):
                for c in range(2):
                    at = 256 * n + 128 * c
                    out[c, o, t, s, :, pl.ds(first, 128)] = result[:, at : at + 128]
        return carry

    lax.fori_loop(0, 6, products, 0)

    for dx in range(4):
        for dz in range(2):
            p_copy(dx, dz, 1, 1, True).wait_recv()

    both = ((0, 0), (0, 1), (1, 0), (1, 1))
    for t in range(2):
        z_copy(t).wait_send()
        for h in range(2):
            for way in range(2):
                y_copy(h, way, t).wait_send()
                f_copy(h, way, t).wait_send()
            for dy in range(4):
                c_copy(h, dy, t).wait_send()
    for t, s in both:
        for dx in range(4):
            for dz in range(2):
                if dx or dz:
                    p_copy(dx, dz, t, s).wait_send()


def last_kernel(done, ops, cols, out, weights, result, sem):
    moves = []
    for c in range(2):
        for o in range(NOP):
            moves.append(pltpu.make_async_copy(done.at[c, o, 0], out.at[c, o, 0], sem.at[c, o, 0]))
            moves.append(pltpu.make_async_copy(done.at[c, o, 1, 0], out.at[c, o, 1, 0], sem.at[c, o, 1]))
    for move in moves:
        move.start()
    real, imag = cols[1, 1, 0], cols[1, 1, 1]
    weights[0:512, 0:512] = real
    weights[0:512, 512:1024] = -imag
    weights[512:1024, 0:512] = imag
    weights[512:1024, 512:1024] = real
    for o in range(NOP):
        for c in range(2):
            for n in range(2):
                rows = slice(512 * c + 256 * n, 512 * c + 256 * n + 256)
                result[c, o, :, 256 * n : 256 * n + 256] = lax.dot_general(
                    ops[1, o], weights[rows, :], (((1,), (1,)), ((), ())), preferred_element_type=jnp.float32
                ).astype(BF16)
            move = pltpu.make_async_copy(result.at[c, o], out.at[c, o, 1, 1], sem.at[c, o, 2])
            move.start()
            moves.append(move)
    for move in moves:
        move.wait()


def shards(perambulator, elementals, op_ids):
    peram = jnp.swapaxes(perambulator, 3, 4)
    dma = pltpu.SemaphoreType.DMA
    vmem = pl.BlockSpec(memory_space=pltpu.VMEM)
    hbm = pl.BlockSpec(memory_space=pl.ANY)
    done, ops, cols = pl.pallas_call(
        kernel,
        out_shape=(
            pltpu.VMEM((2, NOP, 2, 2, 512, 512), BF16),
            pltpu.VMEM((2, NOP, 512, 1024), BF16),
            pltpu.VMEM((2, 2, 2, 512, 512), BF16),
        ),
        in_specs=[pl.BlockSpec(memory_space=pltpu.SMEM), hbm, hbm],
        out_specs=(vmem, vmem, vmem),
        scratch_shapes=[
            pltpu.VMEM((2, 2, 8, 32, 512), BF16),
            pltpu.VMEM((512, 1024), BF16),
            dma(()),
            dma((4, 2, 2, 2)),
            dma((4, 2, 2, 2)),
            dma((2,)),
            dma((2,)),
            dma((2, 2, 2)),
            dma((2, 2, 2)),
            dma((2, 2, 2)),
            dma((2, 2, 2)),
            dma((2, 4, 2)),
            dma((2, 4, 2)),
        ],
        compiler_params=pltpu.CompilerParams(
            collective_id=0, has_side_effects=True, vmem_limit_bytes=12 * 2**20
        ),
    )(pltpu.with_memory_space_constraint(op_ids, pltpu.HBM), pltpu.with_memory_space_constraint(elementals, pltpu.HBM), pltpu.with_memory_space_constraint(peram, pltpu.HBM))
    return pl.pallas_call(
        last_kernel,
        out_shape=jax.ShapeDtypeStruct((2, NOP, 2, 2, 512, 512), BF16),
        in_specs=[vmem, vmem, vmem],
        out_specs=hbm,
        scratch_shapes=[
            pltpu.VMEM((1024, 1024), BF16),
            pltpu.VMEM((2, NOP, 512, 512), BF16),
            dma((2, NOP, 3)),
        ],
        compiler_params=pltpu.CompilerParams(vmem_limit_bytes=16 * 2**20),
    )(
        pltpu.with_memory_space_constraint(done, pltpu.VMEM),
        pltpu.with_memory_space_constraint(ops, pltpu.VMEM),
        pltpu.with_memory_space_constraint(cols, pltpu.VMEM),
    )


def solution(mesh):
    in_specs = (
        P(None, None, "src", None, "sink"),
        P(None, "sink", None, "src", None),
        P("sink", None),
    )
    out_specs = P(None, None, "sink", "src", None, None)
    return jax.shard_map(shards, mesh=mesh, in_specs=in_specs, out_specs=out_specs, check_vma=False)
```

time: 97.6 us -> 74.7 us (0.77)
  Pallas kernels: 91.3 us -> 73.9 us
  local copies, waits for them, and re-layouts: 6.16 us -> 0 us
    pallas_call x1 -> x2, Pallas kernels: 91.3 us -> 73.9 us  [the longest x1 67.9 us: shards(): pl.pallas_call(kernel, out_shape=(pltpu.VMEM((2, NOP, 2, 2, 512, 512), BF...]
    unnamed x1 -> x0, local copies, waits for them, and re-layouts: 6.16 us -> none
where the time goes in v2:
time: 74.7 us; the launch traced here: 73.9 us
  Pallas kernels  73.9 us (99%)
    pallas_call x1, Pallas kernels, shards(): pl.pallas_call(kernel, out_shape=(pltpu.VMEM((2, NOP, 2, 2, 512, 512), BF...  67.9 us
    pallas_call x1, Pallas kernels, shards(): pl.pallas_call(last_kernel, out_shape=jax.ShapeDtypeStruct((2, NOP, 2, 2,...  6.01 us

profile of v2, /device:TPU:1, one launch (start us, length us, event | category | flops | bytes accessed | tf_op | source)
XLA Modules:
  0.0 73.9 jit_solution(5805512545197467212)
XLA Ops:
  0.0 67.9 %shard_map.37 = (bf16[2,4,2,2,512,512]{5,4,3,2,1,0:T(8,128)(2,1)S(1)}, bf16[2,4,512,1024]{3,2,1,0:T(8,128)(2,1)S(1)}, bf16[2,2,2,512,512]{4,3,2,1,0:T(8,128)(2,1)S(1)}) custom-call(s32[2,8]{1,0:T(2,128)} %ids.1, bf16[2,2,8,32,512]{4,3,2,1,0:T(8,128)(2,1)} %stored.1, bf16[2,16,2,64,512]{4,3,2,1,0:T(8,128)(2,1)} %bitcast.1), custom_call_target="tpu_custom_call" | custom-call | tf_op jit(solution)/shard_map/pallas_call | solution.py:208
  67.9 6.0 %shard_map.38 = bf16[2,4,2,2,512,512]{5,4,3,2,1,0:T(8,128)(2,1)} custom-call(bf16[2,4,2,2,512,512]{5,4,3,2,1,0:T(8,128)(2,1)S(1)} %get-tuple-element.8.done, bf16[2,4,512,1024]{3,2,1,0:T(8,128)(2,1)S(1)} %get-tuple-element.9.ops, bf16[2,2,2,512,512]{4,3,2,1,0:T(8,128)(2,1)S(1)} %get-tuple-element.10.cols), custom_call_target="tpu_custom_call" | custom-call | tf_op jit(solution)/shard_map/pallas_call | solution.py:236

commit v3 on v2

--- a/solution.py
+++ b/solution.py
@@ -9,6 +9,7 @@
 
 NOP = 4
 MESH = pl.DeviceIdType.MESH
+HOPS = ((1, 0), (3, 0), (0, 1), (2, 0), (1, 1), (3, 1), (2, 1), (0, 0))
 BF16 = jnp.bfloat16
 
 
@@ -49,8 +50,10 @@
             src_ref=piece, dst_ref=piece, send_sem=send, recv_sem=recv, device_id=(sink, target), device_id_type=MESH
         )
 
-    def z_copy(t, arriving=False):
-        return op_copy(src_of(1, 0, 0) if arriving else src, t, z_send.at[t], z_recv.at[t], src_of(1, 0, 0))
+    def z_copy(t, half, arriving=False):
+        block = src_of(1, 0, 0) if arriving else src
+        part = slice(2 * half, 2 * half + 2)
+        return op_copy(block, t, z_send.at[t, half], z_recv.at[t, half], src_of(1, 0, 0), part)
 
     def y_copy(h, way, t, arriving=False):
         back, to = (3, 1) if way == 0 else (1, 3)
@@ -88,8 +91,8 @@
             y_copy(0, way, t).start()
         c_copy(0, 0, t).start()
 
-    def send_columns(dz, t, s):
-        for dx in (0, 1, 3, 2):
+    def send_columns(t, s):
+        for dx, dz in HOPS:
             p_copy(dx, dz, t, s).start()
 
     def pass_on(h, t):
@@ -98,31 +101,30 @@
             f_copy(h, way, t).start()
             c_copy(h, 3 - 2 * way, t).start()
 
-    z_copy(0).start()
+    z_copy(0, 0).start()
+    z_copy(0, 1).start()
     send_own(0)
-    z_copy(1).start()
+    z_copy(1, 0).start()
+    z_copy(1, 1).start()
     send_own(1)
-    send_columns(1, 0, 0)
-    send_columns(0, 0, 0)
-    for t in range(2):
-        z_copy(t, True).wait_recv()
+    send_columns(0, 0)
+    for t in range(2):
+        z_copy(t, 0, True).wait_recv()
+        z_copy(t, 1, True).wait_recv()
         for way in range(2):
             y_copy(1, way, t).start()
         c_copy(1, 0, t).start()
         pass_on(0, t)
-    send_columns(1, 0, 1)
-    send_columns(0, 0, 1)
+    send_columns(0, 1)
     for t in range(2):
         pass_on(1, t)
-    send_columns(1, 1, 0)
-    send_columns(0, 1, 0)
+    send_columns(1, 0)
     for h in range(2):
         for t in range(2):
             for way in range(2):
                 f_copy(h, way, t, True).wait_recv()
             c_copy(h, 2, t).start()
-    send_columns(1, 1, 1)
-    send_columns(0, 1, 1)
+    send_columns(1, 1)
     for h in range(2):
         for t in range(2):
             for dy in range(4):
@@ -159,7 +161,8 @@
 
     both = ((0, 0), (0, 1), (1, 0), (1, 1))
     for t in range(2):
-        z_copy(t).wait_send()
+        z_copy(t, 0).wait_send()
+        z_copy(t, 1).wait_send()
         for h in range(2):
             for way in range(2):
                 y_copy(h, way, t).wait_send()
@@ -220,8 +223,8 @@
             dma(()),
             dma((4, 2, 2, 2)),
             dma((4, 2, 2, 2)),
-            dma((2,)),
-            dma((2,)),
+            dma((2, 2)),
+            dma((2, 2)),
             dma((2, 2, 2)),
             dma((2, 2, 2)),
             dma((2, 2, 2)),

time: 74.7 us -> 73.6 us (0.985)
  the two profiles are of different devices: /device:TPU:1 before, /device:TPU:0 now
where the time goes in v3:
time: 73.6 us; the launch traced here: 73.5 us
  Pallas kernels  73.5 us (100%)
    pallas_call x1, Pallas kernels, shards(): pl.pallas_call(kernel, out_shape=(pltpu.VMEM((2, NOP, 2, 2, 512, 512), BF...  67.4 us
    pallas_call x1, Pallas kernels, shards(): pl.pallas_call(last_kernel, out_shape=jax.ShapeDtypeStruct((2, NOP, 2, 2,...  6.01 us

profile of v3, /device:TPU:0, one launch (start us, length us, event | category | flops | bytes accessed | tf_op | source)
XLA Modules:
  0.0 73.5 jit_solution(512565367205228424)
XLA Ops:
  0.0 67.4 %shard_map.37 = (bf16[2,4,2,2,512,512]{5,4,3,2,1,0:T(8,128)(2,1)S(1)}, bf16[2,4,512,1024]{3,2,1,0:T(8,128)(2,1)S(1)}, bf16[2,2,2,512,512]{4,3,2,1,0:T(8,128)(2,1)S(1)}) custom-call(s32[2,8]{1,0:T(2,128)} %ids.1, bf16[2,2,8,32,512]{4,3,2,1,0:T(8,128)(2,1)} %stored.1, bf16[2,16,2,64,512]{4,3,2,1,0:T(8,128)(2,1)} %bitcast.1), custom_call_target="tpu_custom_call" | custom-call | tf_op jit(solution)/shard_map/pallas_call | solution.py:211
  67.5 6.0 %shard_map.38 = bf16[2,4,2,2,512,512]{5,4,3,2,1,0:T(8,128)(2,1)} custom-call(bf16[2,4,2,2,512,512]{5,4,3,2,1,0:T(8,128)(2,1)S(1)} %get-tuple-element.8.done, bf16[2,4,512,1024]{3,2,1,0:T(8,128)(2,1)S(1)} %get-tuple-element.9.ops, bf16[2,2,2,512,512]{4,3,2,1,0:T(8,128)(2,1)S(1)} %get-tuple-element.10.cols), custom_call_target="tpu_custom_call" | custom-call | tf_op jit(solution)/shard_map/pallas_call | solution.py:239
